TPU v7x, 32 devices: a whole 2x2x4 slice. The times are simulated.
32 devices in a mesh: segment: 2 (over core), dp: 4 (over z), rows: 4 (over y, x).
Axes of the slice: x: 2, y: 2, z: 4, core: 2. Of those that a mesh axis runs over, the one named last changes fastest.
Arguments:
- latent: bfloat16 [8, 16, 16, 320], P('dp', 'rows'), may hold values from -6 to 6
- hint: bfloat16 [8, 16, 16, 320], P('dp', 'rows'), may hold values from -6 to 6
- decoder_in: bfloat16 [8, 16, 16, 320], P('dp', 'rows'), may hold values from -6 to 6
- target: bfloat16 [8, 16, 16, 320], P('dp', 'rows'), may hold values from -6 to 6
- first_convs: bfloat16 [2, 2, 2880, 320], P('segment', None, 'dp'), may hold values from -0.109375 to 0.109375
- second_convs: bfloat16 [2, 2880, 320], P('segment', 'dp'), may hold values from -0.109375 to 0.109375
- pointwise_weights: bfloat16 [2, 2, 320, 320], P('segment', None, 'dp'), may hold values from -0.3125 to 0.3125
Outputs:
- grad_first: float32 [921600], P(('segment', 'dp', 'rows'))
- grad_zero: float32 [102400], P(('segment', 'dp', 'rows'))
All inputs are finite; a program needn't handle non-finite values.
Results may differ from a plain program's by a relative error of at most 0.0095.
Values may be sent and summed in bfloat16 or wider, within the bound.
No kernel may reach another device: no remote copies, remote signals or barrier semaphores. Data moves between devices by JAX's collectives and lax.ppermute only.
A program may use at most 64 MiB of HBM per device.

v0:
```python
import functools
import math

import jax
import jax.numpy as jnp
from jax import lax
from jax.experimental import pallas as pl
from jax.experimental.pallas import tpu as pltpu
from jax.sharding import PartitionSpec as P

BF16 = jnp.bfloat16
F32 = jnp.float32


def slope(value):
    logistic = 1.0 / (1.0 + jnp.exp(-value))
    return logistic * (1.0 + value * (1.0 - logistic))


def silu(value):
    return value / (1.0 + jnp.exp(-value))


def mm(left, right):
    return jnp.dot(left, right, preferred_element_type=F32)


def spread(wide, sample, values, width):
    cells, channels = values.shape
    height = cells // width
    full = values.astype(F32)
    column = lax.broadcasted_iota(jnp.int32, (cells, channels), 0) % width
    before = jnp.where(column == 0, 0.0, pltpu.roll(full, 1, 0)).astype(BF16)
    after = jnp.where(column == width - 1, 0.0, pltpu.roll(full, cells - 1, 0)).astype(BF16)
    row = jnp.concatenate([before, values, after], axis=1)
    edge = jnp.zeros((width, 3 * channels), BF16)
    wide[sample, 0:width] = edge
    wide[sample, width : width + cells] = row
    wide[sample, width + cells : 2 * width + cells] = edge


def conv(wide, sample, weight, width):
    cells = wide.shape[1] - 2 * width
    depth = wide.shape[2]
    total = None
    for a in range(3):
        part = mm(wide[sample, a * width : a * width + cells], weight[a * depth : (a + 1) * depth])
        total = part if total is None else total + part
    return total


def flip(weight, back):
    channels = weight.shape[1]
    for tap in range(9):
        block = weight[tap * channels : (tap + 1) * channels]
        back[(8 - tap) * channels : (9 - tap) * channels] = block.T


def load(copies, sem):
    handles = [pltpu.make_async_copy(src, dst, sem.at[k]) for k, (src, dst) in enumerate(copies)]
    for handle in handles:
        handle.start()
    for handle in handles:
        handle.wait()


def first_kernel(dims, seg, pair, kernels, points, act, base, held, wide, pre, extra):
    samples, parts, step, width, channels = dims
    cells = parts * step * width

    def whole(which, sample):
        return jnp.concatenate(
            [
                pair[part, which, sample].reshape(step * width, channels)
                for part in range(parts)
            ],
            axis=0,
        )

    @pl.when(seg[0] == 0)
    def _():
        for n in range(samples):
            latent = whole(0, n)
            spread(wide, n, latent, width)
            act[0, n] = silu(conv(wide, n, kernels.at[0], width)).astype(BF16)
            act[1, n] = latent
            mixed = latent.astype(F32) + mm(whole(1, n), points[0])
            mixed = mixed.astype(BF16)
            base[n] = mixed
            spread(wide, n, mixed, width)
            out = conv(wide, n, kernels.at[1], width)
            pre[n] = out
            held[n] = silu(out).astype(BF16)

    @pl.when(seg[0] != 0)
    def _():
        for n in range(samples):
            given = whole(0, n)
            base[n] = whole(1, n)
            spread(wide, n, given, width)
            pre[n] = conv(wide, n, kernels.at[1], width)
            extra[n] = mm(given, points[0])


def second_kernel(dims, seg, sent, held, base, kernels, second, points, proj, out, skip, wide):
    samples, parts, step, width, channels = dims

    @pl.when(seg[0] == 0)
    def _():
        for n in range(samples):
            spread(wide, n, held[n], width)
            value = base[n].astype(F32) + conv(wide, n, second, width)
            value = value.astype(BF16)
            out[n] = value
            proj[n] = mm(value, points[1]).astype(BF16)

    @pl.when(seg[0] != 0)
    def _():
        for n in range(samples):
            spread(wide, n, sent[0, n], width)
            skip[n] = sent[1, n].astype(F32) + conv(wide, n, kernels.at[0], width)


def third_kernel(dims, scale, seg, proj, skip, pre, extra, target, second, points, grad, wide, back):
    samples, parts, step, width, channels = dims

    @pl.when(seg[0] != 0)
    def _():
        flip(second, back)
        for n in range(samples):
            value = (skip[n] + proj[n].astype(F32)).astype(BF16)
            spread(wide, n, value, width)
            before = pre[n] + conv(wide, n, second, width)
            output = silu(before) + extra[n] + mm(value, points[1])
            error = (output - target[n].astype(F32)) * scale
            spread(wide, n, (error * slope(before)).astype(BF16), width)
            total = conv(wide, n, back, width) + mm(error.astype(BF16), points[1].T)
            grad[n] = total.astype(BF16)


def fourth_kernel(dims, seg, grad, base, out, pre, second, points, first, zero, wide, back):
    samples, parts, step, width, channels = dims
    cells = parts * step * width

    @pl.when(seg[0] == 0)
    def _():
        flip(second, back)
        for n in range(samples):
            given = grad[n]
            partial = lax.dot_general(
                out[n], given, (((0,), (0,)), ((), ())), preferred_element_type=F32
            )
            zero[...] = partial if n == 0 else zero[...] + partial
            spread(wide, n, mm(given, points[1].T).astype(BF16), width)
            cot = (conv(wide, n, back, width) * slope(pre[n])).astype(BF16)
            spread(wide, n, base[n], width)
            for a in range(3):
                partial = lax.dot_general(
                    wide[n, a * width : a * width + cells],
                    cot,
                    (((0,), (0,)), ((), ())),
                    preferred_element_type=F32,
                )
                rows = slice(3 * a * channels, 3 * (a + 1) * channels)
                first[rows] = partial if n == 0 else first[rows] + partial

    @pl.when(seg[0] != 0)
    def _():
        first[...] = jnp.zeros(first.shape, F32)
        zero[...] = jnp.zeros(zero.shape, F32)


def call(body, outs, scratch, *args, limit=12, work=0):
    vmem = pl.BlockSpec(memory_space=pltpu.VMEM)
    smem = pl.BlockSpec(memory_space=pltpu.SMEM)
    return pl.pallas_call(
        body,
        out_shape=[jax.ShapeDtypeStruct(shape, dtype) for shape, dtype in outs],
        in_specs=[smem] + [vmem] * (len(args) - 1),
        out_specs=[vmem] * len(outs),
        scratch_shapes=[pltpu.VMEM(shape, dtype) for shape, dtype in scratch],
        compiler_params=pltpu.CompilerParams(vmem_limit_bytes=limit * 1024 * 1024),
        cost_estimate=pl.CostEstimate(flops=work, bytes_accessed=0, transcendentals=0),
    )(*args)


def gathered(block, cut):
    depth, width = block.shape
    parts = lax.axis_size("rows")
    if depth % cut:
        return lax.all_gather(block, "dp", axis=0, tiled=True)
    units = -(-(depth // cut) // parts)
    size = units * cut
    if size * (parts - 1) >= depth:
        return lax.all_gather(block, "dp", axis=0, tiled=True)
    start = jnp.minimum(lax.axis_index("rows") * size, depth - size)
    piece = lax.dynamic_slice_in_dim(block, start, size, 0)
    whole = lax.all_gather(piece, ("dp", "rows"), axis=0, tiled=True)
    if size * parts == depth:
        return whole
    count = lax.axis_size("dp")
    whole = whole.reshape(count, parts, size, width)
    body = whole[:, : parts - 1].reshape(count, (parts - 1) * size, width)
    tail = whole[:, parts - 1, parts * size - depth :]
    return jnp.concatenate([body, tail], axis=1).reshape(count * depth, width)


def role(ids, segment, row):
    return jnp.logical_and(ids[0] == segment, ids[2] == row)


def view(ref, n, cells, channels):
    left = n % 2 * channels
    return ref.at[n // 2 * cells : (n // 2 + 1) * cells, left : left + channels]


def halves(ref):
    rows = ref.shape[0] // 2
    return ref.at[:rows], ref.at[rows:]


def put(piece, base, kern, maps, map_base):
    half, channels = piece.shape[0], kern.shape[1]
    taps, rows = kern.shape[0] // 4, maps.shape[0] // 4
    kern[pl.ds(base, half)] = piece[:, :channels]
    kern[pl.ds(pl.multiple_of(base + half, 16), taps - half)] = piece[: taps - half, channels:]
    maps[pl.ds(map_base, rows)] = piece[taps - half :, channels:]


def place(ids, pieces, kern, maps):
    taps, rows = kern.shape[0] // 4, maps.shape[0] // 4
    inner = jnp.logical_or(ids[1] == 1, ids[1] == 2)
    for k, piece in enumerate(pieces):
        group = lax.bitwise_xor(ids[1], min(k, 3))
        base = pl.multiple_of(group * taps, 16)
        map_base = pl.multiple_of(group * rows, 16)
        if k < 3:
            put(piece, base, kern, maps, map_base)
        else:

            @pl.when(inner if k == 3 else jnp.logical_not(inner))
            def _(piece=piece, base=base, map_base=map_base):
                put(piece, base, kern, maps, map_base)


def early_kernel(width, ids, *refs):
    mine, pieces = refs[:4], refs[4:9]
    images, sent, mixed, bend, sides, kern, maps, wide = refs[9:]
    samples, whole, channels = images.shape[1:]
    act, same = halves(sent)
    for k, part in enumerate(mine):
        cells = part.shape[2] * part.shape[3]
        spot = pl.multiple_of(lax.bitwise_xor(ids[2], k) * cells, 16)
        for which in range(2):
            for n in range(samples):
                images[which, n, pl.ds(spot, cells)] = part[which, n].reshape(cells, channels)

    @pl.when(role(ids, 0, 0))
    def _():
        place(ids, pieces, kern, maps)
        for n in range(samples):
            value = (images[0, n].astype(F32) + mm(images[1, n], maps[...])).astype(BF16)
            view(mixed, n, whole, channels)[...] = value
            view(same, n, whole, channels)[...] = value
            spread(wide, n, value, width)
            out = conv(wide, n, kern, width)
            view(act, n, whole, channels)[...] = silu(out).astype(BF16)
            view(bend, n, whole, channels)[...] = slope(out).astype(BF16)

    @pl.when(role(ids, 0, 3))
    def _():
        place(ids, pieces, kern, maps)
        for n in range(samples):
            latent = images[0, n]
            view(same, n, whole, channels)[...] = latent
            spread(wide, n, latent, width)
            view(act, n, whole, channels)[...] = silu(conv(wide, n, kern, width)).astype(BF16)

    @pl.when(role(ids, 1, 2))
    def _():
        given, extra = halves(sides)
        place(ids, pieces, kern, maps)
        for n in range(samples):
            value = images[0, n]
            spread(wide, n, value, width)
            view(given, n, whole, channels)[...] = conv(wide, n, kern, width).astype(BF16)
            view(extra, n, whole, channels)[...] = mm(value, maps[...]).astype(BF16)


def rows_at(ref, start, extra, count):
    first = pl.multiple_of(start + extra // 8 * 8, 8)
    return ref[pl.ds(first, count + 8)][extra % 8 : extra % 8 + count]


def columns_kernel(width, groups, ids, own, near, below, across, chosen, base, wide, turned):
    @pl.when(ids[0] == 0)
    def _():
        for row, source in enumerate((own, halves(near)[1], below, across)):

            @pl.when(ids[2] == row)
            def _(source=source):
                base[...] = source[...]

        samples, channels = wide.shape[0], wide.shape[2] // 3
        cells = wide.shape[1] - 2 * width
        for n in range(samples):
            spread(wide, n, view(base, n, cells, channels)[...], width)
            for a in range(3):
                turned[
                    3 * a * channels : 3 * (a + 1) * channels, n * cells : (n + 1) * cells
                ] = wide[n, a * width : a * width + cells].astype(F32).T
        block = 9 * channels // (2 * groups)
        share = block // 4
        for row in range(4):

            @pl.when(ids[2] == row)
            def _(row=row):
                for k in range(4):
                    for half in range(2):
                        start = (half * groups + lax.bitwise_xor(ids[1], k)) * block
                        chosen[k, half] = rows_at(
                            turned, start, share * row, chosen.shape[2]
                        ).astype(BF16)


def skip_kernel(width, ids, near, *refs):
    pieces = refs[:5]
    skip, kern, maps, wide = refs[5:]
    samples, channels = wide.shape[0], wide.shape[2] // 3
    cells = wide.shape[1] - 2 * width
    near, latent = halves(near)

    @pl.when(role(ids, 1, 2))
    def _():
        place(ids, pieces, kern, maps)
        for n in range(samples):
            spread(wide, n, view(near, n, cells, channels)[...], width)
            total = view(latent, n, cells, channels)[...].astype(F32) + conv(wide, n, kern, width)
            view(skip, n, cells, channels)[...] = total.astype(BF16)


def layout_kernel(ids, *refs):
    pieces = refs[:5]
    kern, back, maps = refs[5:]

    @pl.when(ids[2] == 1)
    def _():
        place(ids, pieces, kern, maps)

        @pl.when(ids[0] == 1)
        def _():
            flip(kern, back)


def middle_kernel(width, ids, near, kern, maps, out, proj, wide):
    samples, channels = wide.shape[0], wide.shape[2] // 3
    cells = wide.shape[1] - 2 * width
    near, mixed = halves(near)

    @pl.when(role(ids, 0, 1))
    def _():
        for n in range(samples):
            spread(wide, n, view(near, n, cells, channels)[...], width)
            value = view(mixed, n, cells, channels)[...].astype(F32)
            value = (value + conv(wide, n, kern, width)).astype(BF16)
            out[n] = value
            view(proj, n, cells, channels)[...] = mm(value, maps[...]).astype(BF16)


def decoder_kernel(
    width, scale, ids, proj, skip, sides, images, kern, back, maps, grad, turned, wide
):
    samples, cells, channels = images.shape[1:]
    given, extra = halves(sides)

    @pl.when(role(ids, 0, 1))
    def _():
        flip(kern, turned)

    @pl.when(role(ids, 1, 1))
    def _():
        for n in range(samples):

            def part(ref):
                return view(ref, n, cells, channels)[...].astype(F32)

            value = (part(skip) + part(proj)).astype(BF16)
            spread(wide, n, value, width)
            before = part(given) + conv(wide, n, kern, width)
            output = silu(before) + part(extra) + mm(value, maps[...])
            error = (output - images[1, n].astype(F32)) * scale
            spread(wide, n, (error * slope(before)).astype(BF16), width)
            total = conv(wide, n, back, width) + mm(error.astype(BF16), maps[...].T)
            view(grad, n, cells, channels)[...] = total.astype(BF16)


def control_kernel(width, groups, ids, grad, bend, out, turned, maps, parcel, zero, wide):
    @pl.when(role(ids, 0, 1))
    def _():
        samples, cells, channels = out.shape
        for n in range(samples):
            given = view(grad, n, cells, channels)[...]
            partial = lax.dot_general(
                out[n], given, (((0,), (0,)), ((), ())), preferred_element_type=F32
            )
            rows = slice(0, channels)
            zero[rows] = partial if n == 0 else zero[rows] + partial
            spread(wide, n, mm(given, maps[...].T).astype(BF16), width)
            bent = view(bend, n, cells, channels)[...].astype(F32)
            cot = (conv(wide, n, turned, width) * bent).astype(BF16)
            for k in range(4):
                view(parcel.at[k], n, cells, channels)[...] = cot
        block = channels // (2 * groups)
        share = block // 4
        tall = 16
        for k in range(4):
            for other in range(4):
                for half in range(2):
                    start = (half * groups + lax.bitwise_xor(ids[1], other)) * block
                    spot = samples // 2 * cells + other * tall
                    parcel[
                        k, spot : spot + tall, half * channels : (half + 1) * channels
                    ] = rows_at(zero, start, share * (1 ^ k), tall).astype(BF16)


def gradient_kernel(shares, ids, chosen, parcel, first, second, third, kept, sent, taken, flat):
    @pl.when(ids[0] == 0)
    def _():
        for row, source in ((0, first), (1, parcel.at[0]), (2, third), (3, second)):

            @pl.when(ids[2] == row)
            def _(source=source):
                taken[...] = source[...]

        tall, depth = chosen.shape[2], chosen.shape[3]
        channels = flat.shape[1]
        small = 16
        body = depth // 2
        for half in range(2):
            flat[half * body : (half + 1) * body] = taken[
                :body, half * channels : (half + 1) * channels
            ]
        rows = kept.shape[1]
        for k in range(4):
            group = lax.bitwise_xor(ids[1], k)
            spot = body + k * small
            for half, target in enumerate((kept, sent)):
                lanes = slice(half * channels, (half + 1) * channels)
                part = [
                    mm(chosen[k, half], flat[...])[: shares[0]],
                    taken[spot : spot + small, lanes].astype(F32)[: shares[1]],
                    jnp.zeros((2 * rows - sum(shares), channels), F32),
                ]
                value = jnp.concatenate(part, axis=0).astype(target.dtype)
                target[group, :, :channels] = value[:rows]
                target[group, :, channels:] = value[rows:]


def us(time):
    return int(time * 1.15e9)


def hop(values, sizes, moves):
    segments, groups, parts = sizes

    def flat(place):
        return (place[0] * groups + place[1]) * parts + place[2]

    pairs = []
    for s in range(segments):
        for d in range(groups):
            for r in range(parts):
                target = moves(s, d, r)
                if target is not None:
                    pairs.append((flat((s, d, r)), flat(target)))
    return lax.ppermute(values, ("segment", "dp", "rows"), pairs)


def fits(latent, first_convs, pointwise_weights):
    samples, step, width, channels = latent.shape
    taps, maps = first_convs.shape[2], pointwise_weights.shape[2]
    groups, parts = lax.axis_size("dp"), lax.axis_size("rows")
    half = (taps + maps) // 2
    return (
        lax.axis_size("segment") == 2
        and groups == 4
        and parts == 4
        and samples == 2
        and width % 16 == 0
        and taps % 16 == 0
        and maps % 16 == 0
        and half % 16 == 0
        and half <= taps
        and channels % (2 * groups * parts) == 0
        and channels // (2 * groups * parts) <= 16
        and channels // (2 * groups) % 8 == 0
    )


def by_roles(latent, hint, decoder_in, target, first_convs, second_convs, pointwise_weights):
    samples, step, width, channels = latent.shape
    parts, groups = lax.axis_size("rows"), lax.axis_size("dp")
    cells = parts * step * width
    segment, group, row = (lax.axis_index(axis) for axis in ("segment", "dp", "rows"))
    ids = jnp.stack([segment, group, row]).astype(jnp.int32)
    scale = 1.0 / math.sqrt(samples * groups * cells)
    sizes = (lax.axis_size("segment"), groups, parts)
    taps, rows = first_convs.shape[2], pointwise_weights.shape[2]
    plane = (samples, cells, channels)
    pair = (samples // 2 * cells, 2 * channels)
    wide = ((samples, cells + 2 * width, 3 * channels), BF16)
    kern = ((9 * channels, channels), BF16)
    maps = ((channels, channels), BF16)

    kernel = lax.dynamic_index_in_dim(
        first_convs[0], (row % 2 == 0).astype(jnp.int32), 0, keepdims=False
    )
    kernel = jnp.where(row == 1, second_convs[0], kernel)
    half = (taps + rows) // 2

    def pack(kernel, point):
        bundle = jnp.concatenate([kernel, point], axis=0)
        return jnp.concatenate([bundle[:half], bundle[half:]], axis=1)

    packed = pack(kernel, jnp.where(row == 1, pointwise_weights[0, 1], pointwise_weights[0, 0]))
    soon, late = ((0, 0), (0, 3), (1, 2)), ((0, 1), (1, 1))
    homes = soon + late

    first_two = [
        hop(packed, sizes, lambda s, d, r: (s, d ^ k, r) if (s, r) in homes else None)
        for k in (1, 2)
    ]
    mine = jnp.stack(
        [jnp.where(segment == 0, latent, decoder_in), jnp.where(segment == 0, hint, target)]
    )
    others = [hop(mine, sizes, lambda s, d, r: (s, d, r ^ k)) for k in (1, 2, 3)]

    spare, point, packed, *others = lax.optimization_barrier(
        (first_convs[0, 0], pointwise_weights[0, 0], packed, *others)
    )
    other = pack(spare, point)

    def start(values, some):
        return [
            hop(values, sizes, lambda s, d, r: (s, d ^ k, r) if (s, r) in some else None)
            for k in (1, 2)
        ]

    def complete(values, two, some):
        inner = hop(
            values, sizes, lambda s, d, r: (s, d ^ 3, r) if (s, r) in some and d in (1, 2) else None
        )
        outer = hop(
            two[1], sizes, lambda s, d, r: (s, d ^ 1, r) if (s, r) in some and d in (1, 2) else None
        )
        return (values, *two, inner, outer)

    more = start(other, ((1, 2),))
    *first_two, direct = lax.optimization_barrier((*first_two, packed))
    early = complete(direct, first_two, soon)
    twice = jnp.logical_and(segment == 1, row == 2)
    mixture = [jnp.where(twice, a, b) for a, b in ((other, direct), (more[1], first_two[1]))]
    last = complete(mixture[0], [first_two[0], mixture[1]], late + ((1, 2),))
    last = (direct, *first_two, *last[3:])
    later = (other, *more, *last[3:])

    def one_hop(values, *moves):
        table = dict(moves)

        def move(s, d, r):
            target = table.get((s, r))
            return None if target is None else (target[0], d, target[1])

        return hop(values, sizes, move)

    images, sent, mixed, bend, sides = call(
        functools.partial(early_kernel, width),
        [
            ((2,) + plane, BF16),
            ((2 * pair[0], pair[1]), BF16),
            (pair, BF16),
            (pair, BF16),
            ((2 * pair[0], pair[1]), BF16),
        ],
        [kern, maps, wide],
        ids,
        mine,
        *others,
        *early,
        work=us(4.4),
    )
    near = one_hop(sent, ((0, 0), (0, 1)), ((0, 3), (1, 2)))
    below = one_hop(mixed, ((0, 0), (0, 2)))
    across = one_hop(mixed, ((0, 0), (0, 3)))
    bend = one_hop(bend, ((0, 0), (0, 1)))
    sides = one_hop(sides, ((1, 2), (1, 1)))
    kernel, back, point = call(
        layout_kernel, [kern, kern, maps], [], ids, *last, work=us(2)
    )
    kernel, point, near = lax.optimization_barrier((kernel, point, near))
    out, proj = call(
        functools.partial(middle_kernel, width),
        [(plane, BF16), (pair, BF16)],
        [wide],
        ids,
        near,
        kernel,
        point,
        work=us(3),
    )
    proj, near = lax.optimization_barrier((proj, near))
    (skip,) = call(
        functools.partial(skip_kernel, width),
        [(pair, BF16)],
        [kern, maps, wide],
        ids,
        near,
        *later,
        work=us(3.5),
    )
    skip = one_hop(skip, ((1, 2), (1, 1)))
    moved = one_hop(proj, ((0, 1), (1, 1)))
    grad, turned = call(
        functools.partial(decoder_kernel, width, scale),
        [(pair, BF16), kern],
        [wide],
        ids,
        moved,
        skip,
        sides,
        images,
        kernel,
        back,
        point,
        work=us(6),
    )
    tall = -(-(9 * channels // (2 * groups * parts)) // 16) * 16
    (chosen,) = call(
        functools.partial(columns_kernel, width, groups),
        [((4, 2, tall, samples * cells), BF16)],
        [(pair, BF16), wide, ((9 * channels + 24, samples * cells), F32)],
        ids,
        mixed,
        near,
        below,
        across,
        work=us(2),
    )
    grad = one_hop(grad, ((1, 1), (0, 1)))
    grad, chosen = lax.optimization_barrier((grad, chosen))
    body = (pair[0] + 4 * 16, pair[1])
    (parcel,) = call(
        functools.partial(control_kernel, width, groups),
        [((4,) + body, BF16)],
        [((channels + 24, channels), F32), wide],
        ids,
        grad,
        bend,
        out,
        turned,
        point,
        work=us(3.6),
    )
    spread_out = [one_hop(parcel[k], ((0, 1), (0, 1 ^ k))) for k in (1, 2, 3)]
    count = 2 * groups * parts
    shares = (9 * channels // count, channels // count)
    block = (-(-sum(shares) // 32) * 16, 2 * channels)
    kept, sent = call(
        functools.partial(gradient_kernel, shares),
        [((groups,) + block, BF16)] * 2,
        [(body, BF16), ((samples * cells, channels), BF16)],
        ids,
        chosen,
        parcel,
        *spread_out,
    )
    sent = one_hop(sent, *(((0, r), (1, r)) for r in range(parts)))
    sent = jnp.where(segment == 0, kept, sent)
    total = jnp.sum(lax.all_to_all(sent, "dp", 0, 0).astype(F32), axis=0)
    result = jnp.concatenate([total[:, :channels], total[:, channels:]], axis=0)
    flat = result[: sum(shares)].reshape(-1)
    return (flat[: shares[0] * channels], flat[shares[0] * channels :])


def per_device(latent, hint, decoder_in, target, first_convs, second_convs, pointwise_weights):
    if fits(latent, first_convs, pointwise_weights):
        return by_roles(
            latent, hint, decoder_in, target, first_convs, second_convs, pointwise_weights
        )
    samples, step, width, channels = latent.shape
    parts, groups = lax.axis_size("rows"), lax.axis_size("dp")
    cells = parts * step * width
    segment = lax.axis_index("segment")
    seg = segment.reshape(1).astype(jnp.int32)
    scale = 1.0 / math.sqrt(samples * groups * cells)
    dims = (samples, parts, step, width, channels)

    mine = jnp.stack(
        [jnp.where(segment == 0, latent, decoder_in), jnp.where(segment == 0, hint, target)]
    )
    pair = lax.all_gather(mine, "rows")

    taps = first_convs.shape[2]
    maps = pointwise_weights.shape[2]
    stacked = jnp.concatenate(
        [first_convs.reshape(2 * taps, channels), pointwise_weights.reshape(2 * maps, channels)],
        axis=0,
    )
    both = gathered(stacked, 16).reshape(groups, 2 * (taps + maps), channels)
    kernels = jnp.stack(
        [both[:, k * taps : (k + 1) * taps].reshape(groups * taps, channels) for k in range(2)]
    )
    points = jnp.stack(
        [
            both[:, 2 * taps + k * maps : 2 * taps + (k + 1) * maps].reshape(channels, channels)
            for k in range(2)
        ]
    )
    second = gathered(second_convs.reshape(taps, channels), 16)

    plane = (samples, cells, channels)
    wide = ((samples, cells + 2 * width, 3 * channels), BF16)
    back = ((9 * channels, channels), BF16)
    act, base, held, pre, extra = call(
        lambda seg, pair, kernels, points, act, base, held, pre, extra, wide: first_kernel(
            dims, seg, pair, kernels, points, act, base, held, wide, pre, extra
        ),
        [((2,) + plane, BF16), (plane, BF16), (plane, BF16), (plane, F32), (plane, F32)],
        [wide],
        seg,
        pair,
        kernels,
        points,
    )
    sent = lax.ppermute(act, "segment", [(0, 1)])
    proj, out, skip = call(
        functools.partial(second_kernel, dims),
        [(plane, BF16), (plane, BF16), (plane, F32)],
        [wide],
        seg,
        sent,
        held,
        base,
        kernels,
        second,
        points,
    )
    proj = lax.ppermute(proj, "segment", [(0, 1)])
    (grad,) = call(
        functools.partial(third_kernel, dims, scale),
        [(plane, BF16)],
        [wide, back],
        seg,
        proj,
        skip,
        pre,
        extra,
        base,
        second,
        points,
    )
    grad = lax.ppermute(grad, "segment", [(1, 0)])
    first, zero = call(
        functools.partial(fourth_kernel, dims),
        [((9 * channels, channels), F32), ((channels, channels), F32)],
        [wide, back],
        seg,
        grad,
        base,
        out,
        pre,
        second,
        points,
    )
    once = lax.axis_index("rows") == 0
    axes = ("segment", "dp", "rows")
    return tuple(
        lax.psum_scatter(
            jnp.where(once, value, 0.0).reshape(-1), axes, scatter_dimension=0, tiled=True
        )
        for value in (first, zero)
    )


def solution(mesh):
    spread_out = P("dp", "rows", None, None)
    placed = (
        spread_out,
        spread_out,
        spread_out,
        spread_out,
        P("segment", None, "dp", None),
        P("segment", "dp", None),
        P("segment", None, "dp", None),
    )
    return jax.shard_map(
        per_device,
        mesh=mesh,
        in_specs=placed,
        out_specs=(P(("segment", "dp", "rows")), P(("segment", "dp", "rows"))),
        check_vma=False,
    )
```

profile of v0, /device:TPU:4, one launch (start us, length us, event | category | flops | bytes accessed | tf_op | source)
XLA Modules:
  0.0 118.1 jit_solution(7771540487436885253)
XLA Ops:
  0.7 2.1 %fusion.3 = (bf16[1,1,720,320]{2,3,1,0:T(8,128)(2,1)}, bf16[1,1,720,320]{2,3,1,0:T(8,128)(2,1)S(1)}) fusion(bf16[1,2,720,320]{2,3,1,0:T(8,128)(2,1)} %param.11, s32[]{:T(128)S(6)} %select_n.62), kind=kLoop, calls=%fused_computation.20 | loop fusion | bytes 1843204 | tf_op jit(solution)/shard_map/slice | solution.py:539
  3.8 0.7 collective-permute-start
  4.5 0.7 collective-permute-start.1
  5.4 8.2 %collective-permute-start.2 = (bf16[2,2,4,16,320]{4,3,2,1,0:T(8,128)(2,1)S(1)}, bf16[2,2,4,16,320]{4,3,2,1,0:T(8,128)(2,1)S(1)}, u32[]{:S(2)}, u32[]{:S(2)}) collective-permute-start(bf16[2,2,4,16,320]{4,3,2,1,0:T(8,128)(2,1)S(1)} %pad_maximum_fusion.2.refs_0_), channel_id=1, source_target_pairs={{0,1},{1,0},{2,3},{3,2},{4,5},{5,4},{6,7},{7,6},{8,9},{9,8},{10,11... | collective-permute-start | bytes 491528 | tf_op jit(solution)/shard_map/ppermute | solution.py:476
  14.0 1.0 collective-permute-start.4
  15.0 1.3 %copy.12 = bf16[1,1,720,320]{3,2,1,0:T(8,128)(2,1)S(1)} copy(bf16[1,1,720,320]{2,3,1,0:T(8,128)(2,1)} %get-tuple-element.67) | data formatting | bytes 921600
  16.4 2.9 %collective-permute-done.2.refs_1_ = bf16[2,2,4,16,320]{4,3,2,1,0:T(8,128)(2,1)S(1)} collective-permute-done((bf16[2,2,4,16,320]{4,3,2,1,0:T(8,128)(2,1)S(1)}, bf16[2,2,4,16,320]{4,3,2,1,0:T(8,128)(2,1)S(1)}, u32[]{:S(2)}, u32[]{:S(2)}) %collective-permute-start.2) | collective-permute-done | bytes 163872 | tf_op jit(solution)/shard_map/ppermute | solution.py:476
  19.3 3.7 %collective-permute-done.3.refs_2_ = bf16[2,2,4,16,320]{4,3,2,1,0:T(8,128)(2,1)S(1)} collective-permute-done((bf16[2,2,4,16,320]{4,3,2,1,0:T(8,128)(2,1)S(1)}, bf16[2,2,4,16,320]{4,3,2,1,0:T(8,128)(2,1)S(1)}, u32[]{:S(2)}, u32[]{:S(2)}) %collective-permute-start.3) | collective-permute-done | bytes 163872 | tf_op jit(solution)/shard_map/ppermute | solution.py:476
  23.0 2.1 %broadcast_select_fusion.1 = (bf16[400,640]{1,0:T(8,128)(2,1)}, bf16[400,640]{1,0:T(8,128)(2,1)S(1)}) fusion(bf16[400,640]{1,0:T(8,128)(2,1)S(1)} %fusion.1.refs_0_.refs_4_, pred[]{:T(512)S(6)} %and.12, bf16[80,320]{1,0:T(8,128)(2,1)S(1)} %slice_bitcast_fusion.3, bf16[720,320]{1,0:T(8,128)(2,1)} %bitcast.25, bf16[400,320]{1,0:T(8,128)(2,1)S(1)} %slice.59), kind=kLoop, calls=%fused_computation.7 | loop fusion | flops 1792000 | bytes 2304001 | tf_op jit(solution)/shard_map/jit(_where)/select_n | solution.py:562
  25.8 0.7 collective-permute-start.8
  26.5 1.5 %collective-permute-start.9 = (bf16[400,640]{1,0:T(8,128)(2,1)S(1)}, bf16[400,640]{1,0:T(8,128)(2,1)}, u32[]{:S(2)}, u32[]{:S(2)}) collective-permute-start(bf16[400,640]{1,0:T(8,128)(2,1)S(1)} %collective-permute-done.1.refs_2_.refs_6_), channel_id=1, source_target_pairs={{4,0},{7,3},{8,12},{11,15},{22,18},{26,30}} | collective-permute-start | bytes 1536008 | tf_op jit(solution)/shard_map/ppermute | solution.py:476
  28.1 0.7 collective-permute-start.5
  28.8 0.7 collective-permute-start.7
  29.6 0.9 copy-done.1
  30.5 0.9 copy-done.3
  31.4 1.1 shard_map.87
  32.6 0.7 collective-permute-start.10
  33.3 0.7 collective-permute-start.12
  34.0 0.7 collective-permute-start.14
  34.7 0.7 shard_map.86
  38.0 1.3 %collective-permute-start.16 = (bf16[256,640]{1,0:T(8,128)(2,1)S(1)}, bf16[256,640]{1,0:T(8,128)(2,1)S(1)}, u32[]{:S(2)}, u32[]{:S(2)}) collective-permute-start(bf16[256,640]{1,0:T(8,128)(2,1)S(1)} %get-tuple-element.54.own), channel_id=1, source_target_pairs={{0,2},{4,6},{8,10},{12,14}} | collective-permute-start | bytes 983048 | tf_op jit(solution)/shard_map/ppermute | solution.py:476
  41.9 23.2 %collective-permute-done.16.below = bf16[256,640]{1,0:T(8,128)(2,1)S(1)} collective-permute-done((bf16[256,640]{1,0:T(8,128)(2,1)S(1)}, bf16[256,640]{1,0:T(8,128)(2,1)S(1)}, u32[]{:S(2)}, u32[]{:S(2)}) %collective-permute-start.16) | collective-permute-done | bytes 327712 | tf_op jit(solution)/shard_map/ppermute | solution.py:476
  65.1 2.1 %shard_map.91.chosen = bf16[4,2,96,512]{3,2,1,0:T(8,128)(2,1)S(1)} custom-call(s32[3]{0:T(128)S(1)} %pad_add_fusion.ids, bf16[256,640]{1,0:T(8,128)(2,1)S(1)} %get-tuple-element.54.own, bf16[512,640]{1,0:T(8,128)(2,1)S(1)} %collective-permute-done.10.near, bf16[256,640]{1,0:T(8,128)(2,1)S(1)} %collective-permute-done.16.below, ...), custom_call_target="tpu_custom_call" | custom-call | flops 2300000000 | tf_op jit(solution)/shard_map/pallas_call | solution.py:176
  67.9 0.7 collective-permute-start.19
  68.6 0.7 collective-permute-start.20
  69.3 1.3 %collective-permute-start.21 = (bf16[320,640]{1,0:T(8,128)(2,1)S(1)}, bf16[320,640]{1,0:T(8,128)(2,1)S(1)}, u32[]{:S(2)}, u32[]{:S(2)}) collective-permute-start(bf16[320,640]{1,0:T(8,128)(2,1)S(1)} %get-tuple-element.64), channel_id=1, source_target_pairs={{1,2},{5,6},{9,10},{13,14}} | collective-permute-start | bytes 1228808 | tf_op jit(solution)/shard_map/ppermute | solution.py:476
  70.7 27.3 %collective-permute-done.21.third = bf16[320,640]{1,0:T(8,128)(2,1)S(1)} collective-permute-done((bf16[320,640]{1,0:T(8,128)(2,1)S(1)}, bf16[320,640]{1,0:T(8,128)(2,1)S(1)}, u32[]{:S(2)}, u32[]{:S(2)}) %collective-permute-start.21) | collective-permute-done | bytes 409632 | tf_op jit(solution)/shard_map/ppermute | solution.py:476
  98.0 1.4 %shard_map.93 = (bf16[4,64,640]{2,1,0:T(8,128)(2,1)S(1)}, bf16[4,64,640]{2,1,0:T(8,128)(2,1)S(1)}) custom-call(s32[3]{0:T(128)S(1)} %pad_add_fusion.ids, bf16[4,2,96,512]{3,2,1,0:T(8,128)(2,1)S(1)} %shard_map.91.chosen, bf16[4,320,640]{2,1,0:T(8,128)(2,1)S(1)} %shard_map.92.parcel, bf16[320,640]{1,0:T(8,128)(2,1)S(1)} %collective-permute-done.19.first, ...), custom_call_target="tpu_custom_call" | custom-call | tf_op jit(solution)/shard_map/pallas_call | solution.py:176
  99.4 1.3 %collective-permute-start.22 = (bf16[4,64,640]{2,1,0:T(8,128)(2,1)S(1)}, bf16[4,64,640]{2,1,0:T(8,128)(2,1)S(1)}, u32[]{:S(2)}, u32[]{:S(2)}) collective-permute-start(bf16[4,64,640]{2,1,0:T(8,128)(2,1)S(1)} %get-tuple-element.61), channel_id=1, source_target_pairs={{0,16},{1,17},{2,18},{3,19},{4,20},{5,21},{6,22},{7,23},{8,24},{9,... | collective-permute-start | bytes 983048 | tf_op jit(solution)/shard_map/ppermute | solution.py:476
  100.8 1.2 %collective-permute-done.22 = bf16[4,64,640]{2,1,0:T(8,128)(2,1)S(1)} collective-permute-done((bf16[4,64,640]{2,1,0:T(8,128)(2,1)S(1)}, bf16[4,64,640]{2,1,0:T(8,128)(2,1)S(1)}, u32[]{:S(2)}, u32[]{:S(2)}) %collective-permute-start.22) | collective-permute-done | bytes 327712 | tf_op jit(solution)/shard_map/ppermute | solution.py:476
  102.0 14.4 %all_to_all.5 = bf16[4,64,640]{2,1,0:T(8,128)(2,1)S(1)} all-to-all(bf16[4,64,640]{2,1,0:T(8,128)(2,1)S(1)} %broadcast_select_fusion.2), channel_id=1, replica_groups=mesh['segment'=2,'dp'=4,'rows'=4] {'dp'}, dimensions={0} | all-to-all | bytes 655360 | tf_op jit(solution)/shard_map/all_to_all | solution.py:679
  116.6 0.8 slice.67
  (68 shorter events, 9.2 us)
Async XLA Ops:
  0.6 2.4 %copy-start.5 = (bf16[1,720,320]{1,2,0:T(8,128)(2,1)S(1)}, bf16[1,720,320]{1,2,0:T(8,128)(2,1)}, u32[]{:S(2)}) copy-start(bf16[1,720,320]{1,2,0:T(8,128)(2,1)} %param.12) | copy-start | bytes 1382404
  3.0 2.2 %copy-start.7 = (bf16[2,4,16,320]{3,2,1,0:T(8,128)(2,1)S(1)}, bf16[2,4,16,320]{3,2,1,0:T(8,128)(2,1)}, u32[]{:S(2)}) copy-start(bf16[2,4,16,320]{3,2,1,0:T(8,128)(2,1)} %param.8) | copy-start | bytes 245764
  3.0 2.2 %copy-start.8 = (bf16[2,4,16,320]{3,2,1,0:T(8,128)(2,1)S(1)}, bf16[2,4,16,320]{3,2,1,0:T(8,128)(2,1)}, u32[]{:S(2)}) copy-start(bf16[2,4,16,320]{3,2,1,0:T(8,128)(2,1)} %param.10) | copy-start | bytes 245764
  3.1 2.2 %copy-start.9 = (bf16[2,4,16,320]{3,2,1,0:T(8,128)(2,1)S(1)}, bf16[2,4,16,320]{3,2,1,0:T(8,128)(2,1)}, u32[]{:S(2)}) copy-start(bf16[2,4,16,320]{3,2,1,0:T(8,128)(2,1)} %param.7) | copy-start | bytes 245764
  3.1 2.2 %copy-start.10 = (bf16[2,4,16,320]{3,2,1,0:T(8,128)(2,1)S(1)}, bf16[2,4,16,320]{3,2,1,0:T(8,128)(2,1)}, u32[]{:S(2)}) copy-start(bf16[2,4,16,320]{3,2,1,0:T(8,128)(2,1)} %param.9) | copy-start | bytes 245764
  3.8 19.2 %collective-permute-start = (bf16[400,640]{1,0:T(8,128)(2,1)S(1)}, bf16[400,640]{1,0:T(8,128)(2,1)S(1)}, u32[]{:S(2)}, u32[]{:S(2)}) collective-permute-start(bf16[400,640]{1,0:T(8,128)(2,1)S(1)} %fusion.1.refs_0_.refs_4_), channel_id=1, source_target_pairs={{0,4},{1,5},{3,7},{4,0},{5,1},{7,3},{8,12},{9,13},{11,15},{12,8},{... | collective-permute-start | bytes 1536008 | tf_op jit(solution)/shard_map/ppermute | solution.py:476
  4.5 18.5 %collective-permute-start.1 = (bf16[400,640]{1,0:T(8,128)(2,1)S(1)}, bf16[400,640]{1,0:T(8,128)(2,1)S(1)}, u32[]{:S(2)}, u32[]{:S(2)}) collective-permute-start(bf16[400,640]{1,0:T(8,128)(2,1)S(1)} %fusion.1.refs_0_.refs_4_), channel_id=1, source_target_pairs={{0,8},{1,9},{3,11},{4,12},{5,13},{7,15},{8,0},{9,1},{11,3},{12,4},... | collective-permute-start | bytes 1536008 | tf_op jit(solution)/shard_map/ppermute | solution.py:476
  5.4 13.9 %collective-permute-start.2 = (bf16[2,2,4,16,320]{4,3,2,1,0:T(8,128)(2,1)S(1)}, bf16[2,2,4,16,320]{4,3,2,1,0:T(8,128)(2,1)S(1)}, u32[]{:S(2)}, u32[]{:S(2)}) collective-permute-start(bf16[2,2,4,16,320]{4,3,2,1,0:T(8,128)(2,1)S(1)} %pad_maximum_fusion.2.refs_0_), channel_id=1, source_target_pairs={{0,1},{1,0},{2,3},{3,2},{4,5},{5,4},{6,7},{7,6},{8,9},{9,8},{10,11... | collective-permute-start | bytes 491528 | tf_op jit(solution)/shard_map/ppermute | solution.py:476
  13.5 9.4 %collective-permute-start.3 = (bf16[2,2,4,16,320]{4,3,2,1,0:T(8,128)(2,1)S(1)}, bf16[2,2,4,16,320]{4,3,2,1,0:T(8,128)(2,1)S(1)}, u32[]{:S(2)}, u32[]{:S(2)}) collective-permute-start(bf16[2,2,4,16,320]{4,3,2,1,0:T(8,128)(2,1)S(1)} %pad_maximum_fusion.2.refs_0_), channel_id=1, source_target_pairs={{0,2},{1,3},{2,0},{3,1},{4,6},{5,7},{6,4},{7,5},{8,10},{9,11},{10,... | collective-permute-start | bytes 491528 | tf_op jit(solution)/shard_map/ppermute | solution.py:476
  14.0 8.9 %collective-permute-start.4 = (bf16[2,2,4,16,320]{4,3,2,1,0:T(8,128)(2,1)S(1)}, bf16[2,2,4,16,320]{4,3,2,1,0:T(8,128)(2,1)S(1)}, u32[]{:S(2)}, u32[]{:S(2)}) collective-permute-start(bf16[2,2,4,16,320]{4,3,2,1,0:T(8,128)(2,1)S(1)} %pad_maximum_fusion.2.refs_0_), channel_id=1, source_target_pairs={{0,3},{1,2},{2,1},{3,0},{4,7},{5,6},{6,5},{7,4},{8,11},{9,10},{10,... | collective-permute-start | bytes 491528 | tf_op jit(solution)/shard_map/ppermute | solution.py:476
  16.4 6.6 %copy-start.4 = (bf16[1,1,720,320]{3,2,1,0:T(8,128)(2,1)}, bf16[1,1,720,320]{3,2,1,0:T(8,128)(2,1)S(1)}, u32[]{:S(2)}) copy-start(bf16[1,1,720,320]{3,2,1,0:T(8,128)(2,1)S(1)} %copy.12) | copy-start | bytes 1382404
  22.9 2.2 %copy-start = (bf16[2,2,4,16,320]{4,3,2,1,0:T(8,128)(2,1)}, bf16[2,2,4,16,320]{4,3,2,1,0:T(8,128)(2,1)S(1)}, u32[]{:S(2)}) copy-start(bf16[2,2,4,16,320]{4,3,2,1,0:T(8,128)(2,1)S(1)} %collective-permute-done.3.refs_2_) | copy-start | bytes 491524
  22.9 2.2 %copy-start.2 = (bf16[2,2,4,16,320]{4,3,2,1,0:T(8,128)(2,1)}, bf16[2,2,4,16,320]{4,3,2,1,0:T(8,128)(2,1)S(1)}, u32[]{:S(2)}) copy-start(bf16[2,2,4,16,320]{4,3,2,1,0:T(8,128)(2,1)S(1)} %collective-permute-done.4.refs_3_) | copy-start | bytes 491524
  25.1 3.6 %collective-permute-start.6 = (bf16[400,640]{1,0:T(8,128)(2,1)S(1)}, bf16[400,640]{1,0:T(8,128)(2,1)S(1)}, u32[]{:S(2)}, u32[]{:S(2)}) collective-permute-start(bf16[400,640]{1,0:T(8,128)(2,1)S(1)} %get-tuple-element.63.refs_0_), channel_id=1, source_target_pairs={{18,26},{22,30},{26,18},{30,22}} | collective-permute-start | bytes 1536008 | tf_op jit(solution)/shard_map/ppermute | solution.py:476
  25.8 3.7 %collective-permute-start.8 = (bf16[400,640]{1,0:T(8,128)(2,1)S(1)}, bf16[400,640]{1,0:T(8,128)(2,1)S(1)}, u32[]{:S(2)}, u32[]{:S(2)}) collective-permute-start(bf16[400,640]{1,0:T(8,128)(2,1)S(1)} %fusion.1.refs_0_.refs_4_), channel_id=1, source_target_pairs={{4,8},{7,11},{8,4},{11,7},{22,26},{26,22}} | collective-permute-start | bytes 1536008 | tf_op jit(solution)/shard_map/ppermute | solution.py:476
  26.5 3.0 %collective-permute-start.9 = (bf16[400,640]{1,0:T(8,128)(2,1)S(1)}, bf16[400,640]{1,0:T(8,128)(2,1)}, u32[]{:S(2)}, u32[]{:S(2)}) collective-permute-start(bf16[400,640]{1,0:T(8,128)(2,1)S(1)} %collective-permute-done.1.refs_2_.refs_6_), channel_id=1, source_target_pairs={{4,0},{7,3},{8,12},{11,15},{22,18},{26,30}} | collective-permute-start | bytes 1536008 | tf_op jit(solution)/shard_map/ppermute | solution.py:476
  28.1 6.6 %collective-permute-start.5 = (bf16[400,640]{1,0:T(8,128)(2,1)}, bf16[400,640]{1,0:T(8,128)(2,1)S(1)}, u32[]{:S(2)}, u32[]{:S(2)}) collective-permute-start(bf16[400,640]{1,0:T(8,128)(2,1)} %get-tuple-element.62), channel_id=1, source_target_pairs={{5,9},{9,5},{21,25},{22,26},{25,21},{26,22}} | collective-permute-start | bytes 1536008 | tf_op jit(solution)/shard_map/ppermute | solution.py:476
  28.8 5.9 %collective-permute-start.7 = (bf16[400,640]{1,0:T(8,128)(2,1)S(1)}, bf16[400,640]{1,0:T(8,128)(2,1)S(1)}, u32[]{:S(2)}, u32[]{:S(2)}) collective-permute-start(bf16[400,640]{1,0:T(8,128)(2,1)S(1)} %broadcast_select_fusion), channel_id=1, source_target_pairs={{5,1},{9,13},{21,17},{22,18},{25,29},{26,30}} | collective-permute-start | bytes 1536008 | tf_op jit(solution)/shard_map/ppermute | solution.py:476
  29.6 0.9 copy-start.1
  32.6 2.9 %collective-permute-start.10 = (bf16[512,640]{1,0:T(8,128)(2,1)S(1)}, bf16[512,640]{1,0:T(8,128)(2,1)S(1)}, u32[]{:S(2)}, u32[]{:S(2)}) collective-permute-start(bf16[512,640]{1,0:T(8,128)(2,1)S(1)} %get-tuple-element.43), channel_id=1, source_target_pairs={{0,1},{3,18},{4,5},{7,22},{8,9},{11,26},{12,13},{15,30}} | collective-permute-start | bytes 1966088 | tf_op jit(solution)/shard_map/ppermute | solution.py:476
  33.3 2.7 %collective-permute-start.12 = (bf16[400,640]{1,0:T(8,128)(2,1)S(1)}, bf16[400,640]{1,0:T(8,128)(2,1)S(1)}, u32[]{:S(2)}, u32[]{:S(2)}) collective-permute-start(bf16[400,640]{1,0:T(8,128)(2,1)S(1)} %get-tuple-element.63.refs_0_), channel_id=1, source_target_pairs={{18,22},{22,18},{26,30},{30,26}} | collective-permute-start | bytes 1536008 | tf_op jit(solution)/shard_map/ppermute | solution.py:476
  34.0 6.0 %collective-permute-start.14 = (bf16[512,640]{1,0:T(8,128)(2,1)S(1)}, bf16[512,640]{1,0:T(8,128)(2,1)S(1)}, u32[]{:S(2)}, u32[]{:S(2)}) collective-permute-start(bf16[512,640]{1,0:T(8,128)(2,1)S(1)} %get-tuple-element.50), channel_id=1, source_target_pairs={{18,17},{22,21},{26,25},{30,29}} | collective-permute-start | bytes 1966088 | tf_op jit(solution)/shard_map/ppermute | solution.py:476
  36.6 3.4 %collective-permute-start.13 = (bf16[256,640]{1,0:T(8,128)(2,1)S(1)}, bf16[256,640]{1,0:T(8,128)(2,1)S(1)}, u32[]{:S(2)}, u32[]{:S(2)}) collective-permute-start(bf16[256,640]{1,0:T(8,128)(2,1)S(1)} %shard_map.89), channel_id=1, source_target_pairs={{18,17},{22,21},{26,25},{30,29}} | collective-permute-start | bytes 983048 | tf_op jit(solution)/shard_map/ppermute | solution.py:476
  37.3 2.7 %collective-permute-start.11 = (bf16[256,640]{1,0:T(8,128)(2,1)S(1)}, bf16[256,640]{1,0:T(8,128)(2,1)S(1)}, u32[]{:S(2)}, u32[]{:S(2)}) collective-permute-start(bf16[256,640]{1,0:T(8,128)(2,1)S(1)} %get-tuple-element.48), channel_id=1, source_target_pairs={{1,17},{5,21},{9,25},{13,29}} | collective-permute-start | bytes 983048 | tf_op jit(solution)/shard_map/ppermute | solution.py:476
  38.0 27.2 %collective-permute-start.16 = (bf16[256,640]{1,0:T(8,128)(2,1)S(1)}, bf16[256,640]{1,0:T(8,128)(2,1)S(1)}, u32[]{:S(2)}, u32[]{:S(2)}) collective-permute-start(bf16[256,640]{1,0:T(8,128)(2,1)S(1)} %get-tuple-element.54.own), channel_id=1, source_target_pairs={{0,2},{4,6},{8,10},{12,14}} | collective-permute-start | bytes 983048 | tf_op jit(solution)/shard_map/ppermute | solution.py:476
  39.3 25.9 %collective-permute-start.17 = (bf16[256,640]{1,0:T(8,128)(2,1)S(1)}, bf16[256,640]{1,0:T(8,128)(2,1)S(1)}, u32[]{:S(2)}, u32[]{:S(2)}) collective-permute-start(bf16[256,640]{1,0:T(8,128)(2,1)S(1)} %get-tuple-element.54.own), channel_id=1, source_target_pairs={{0,3},{4,7},{8,11},{12,15}} | collective-permute-start | bytes 983048 | tf_op jit(solution)/shard_map/ppermute | solution.py:476
  40.5 26.7 %collective-permute-start.15 = (bf16[256,640]{1,0:T(8,128)(2,1)S(1)}, bf16[256,640]{1,0:T(8,128)(2,1)S(1)}, u32[]{:S(2)}, u32[]{:S(2)}) collective-permute-start(bf16[256,640]{1,0:T(8,128)(2,1)S(1)} %get-tuple-element.53), channel_id=1, source_target_pairs={{17,1},{21,5},{25,9},{29,13}} | collective-permute-start | bytes 983048 | tf_op jit(solution)/shard_map/ppermute | solution.py:476
  41.2 26.0 %collective-permute-start.18 = (bf16[256,640]{1,0:T(8,128)(2,1)S(1)}, bf16[256,640]{1,0:T(8,128)(2,1)S(1)}, u32[]{:S(2)}, u32[]{:S(2)}) collective-permute-start(bf16[256,640]{1,0:T(8,128)(2,1)S(1)} %get-tuple-element.57), channel_id=1, source_target_pairs={{0,1},{4,5},{8,9},{12,13}} | collective-permute-start | bytes 983048 | tf_op jit(solution)/shard_map/ppermute | solution.py:476
  67.9 2.7 %collective-permute-start.19 = (bf16[320,640]{1,0:T(8,128)(2,1)S(1)}, bf16[320,640]{1,0:T(8,128)(2,1)S(1)}, u32[]{:S(2)}, u32[]{:S(2)}) collective-permute-start(bf16[320,640]{1,0:T(8,128)(2,1)S(1)} %get-tuple-element.66), channel_id=1, source_target_pairs={{1,0},{5,4},{9,8},{13,12}} | collective-permute-start | bytes 1228808 | tf_op jit(solution)/shard_map/ppermute | solution.py:476
  68.6 2.0 %collective-permute-start.20 = (bf16[320,640]{1,0:T(8,128)(2,1)S(1)}, bf16[320,640]{1,0:T(8,128)(2,1)S(1)}, u32[]{:S(2)}, u32[]{:S(2)}) collective-permute-start(bf16[320,640]{1,0:T(8,128)(2,1)S(1)} %get-tuple-element.65), channel_id=1, source_target_pairs={{1,3},{5,7},{9,11},{13,15}} | collective-permute-start | bytes 1228808 | tf_op jit(solution)/shard_map/ppermute | solution.py:476
  69.3 28.6 %collective-permute-start.21 = (bf16[320,640]{1,0:T(8,128)(2,1)S(1)}, bf16[320,640]{1,0:T(8,128)(2,1)S(1)}, u32[]{:S(2)}, u32[]{:S(2)}) collective-permute-start(bf16[320,640]{1,0:T(8,128)(2,1)S(1)} %get-tuple-element.64), channel_id=1, source_target_pairs={{1,2},{5,6},{9,10},{13,14}} | collective-permute-start | bytes 1228808 | tf_op jit(solution)/shard_map/ppermute | solution.py:476
  99.4 2.5 %collective-permute-start.22 = (bf16[4,64,640]{2,1,0:T(8,128)(2,1)S(1)}, bf16[4,64,640]{2,1,0:T(8,128)(2,1)S(1)}, u32[]{:S(2)}, u32[]{:S(2)}) collective-permute-start(bf16[4,64,640]{2,1,0:T(8,128)(2,1)S(1)} %get-tuple-element.61), channel_id=1, source_target_pairs={{0,16},{1,17},{2,18},{3,19},{4,20},{5,21},{6,22},{7,23},{8,24},{9,... | collective-permute-start | bytes 983048 | tf_op jit(solution)/shard_map/ppermute | solution.py:476
  (2 other events, 1.8 us)
where the time goes:
time: 119 us; the launch traced here: 118 us
  waiting for transfers between devices  58.3 us (49%)
  starting transfers between devices  26.1 us (22%)
  blocking collectives  14.4 us (12%)
  local copies, waits for them, and re-layouts  7.76 us (7%)
  Pallas kernels  7.63 us (6%)
  other arithmetic  2.71 us (2%)
  between operations  1.2 us (1%)
    ppermute x23, waiting for transfers between devices, hop(): return lax.ppermute(values, ('segment', 'dp', 'rows'), pairs)  58.3 us
    ppermute x23, starting transfers between devices, hop(): return lax.ppermute(values, ('segment', 'dp', 'rows'), pairs)  26.1 us
    all_to_all x1, blocking collectives, by_roles(): total = jnp.sum(lax.all_to_all(sent, 'dp', 0, 0).astype(F32), axis=0)  14.4 us
    pallas_call x8, Pallas kernels, call(): pl.pallas_call(body, out_shape=[jax.ShapeDtypeStruct(shape, dtype) for sh...  7.63 us
    unnamed x24, local copies, waits for them, and re-layouts  3.63 us
  transfers between devices with their start and end apart: 23, of which 5 were waited for; matrix products, arithmetic and copies ran while one was open for 1% of the time, Pallas kernels for 5%

commit v1 on v0

--- a/solution.py
+++ b/solution.py
@@ -234,7 +234,7 @@
         group = lax.bitwise_xor(ids[1], min(k, 3))
         base = pl.multiple_of(group * taps, 16)
         map_base = pl.multiple_of(group * rows, 16)
-        if k < 3:
+        if k < 3 or len(pieces) == 4:
             put(piece, base, kern, maps, map_base)
         else:
 
@@ -244,8 +244,8 @@
 
 
 def early_kernel(width, ids, *refs):
-    mine, pieces = refs[:4], refs[4:9]
-    images, sent, mixed, bend, sides, kern, maps, wide = refs[9:]
+    mine, pieces = refs[:4], refs[4:8]
+    images, sent, mixed, bend, kern, maps, wide = refs[8:]
     samples, whole, channels = images.shape[1:]
     act, same = halves(sent)
     for k, part in enumerate(mine):
@@ -276,15 +276,21 @@
             spread(wide, n, latent, width)
             view(act, n, whole, channels)[...] = silu(conv(wide, n, kern, width)).astype(BF16)
 
+
+def given_kernel(width, ids, images, *refs):
+    pieces = refs[:4]
+    sides, kern, maps, wide = refs[4:]
+    samples, cells, channels = images.shape[1:]
+    given, extra = halves(sides)
+
     @pl.when(role(ids, 1, 2))
     def _():
-        given, extra = halves(sides)
         place(ids, pieces, kern, maps)
         for n in range(samples):
             value = images[0, n]
             spread(wide, n, value, width)
-            view(given, n, whole, channels)[...] = conv(wide, n, kern, width).astype(BF16)
-            view(extra, n, whole, channels)[...] = mm(value, maps[...]).astype(BF16)
+            view(given, n, cells, channels)[...] = conv(wide, n, kern, width).astype(BF16)
+            view(extra, n, cells, channels)[...] = mm(value, maps[...]).astype(BF16)
 
 
 def rows_at(ref, start, extra, count):
@@ -324,8 +330,8 @@
 
 
 def skip_kernel(width, ids, near, *refs):
-    pieces = refs[:5]
-    skip, kern, maps, wide = refs[5:]
+    pieces = refs[:4]
+    skip, kern, maps, wide = refs[4:]
     samples, channels = wide.shape[0], wide.shape[2] // 3
     cells = wide.shape[1] - 2 * width
     near, latent = halves(near)
@@ -339,7 +345,7 @@
             view(skip, n, cells, channels)[...] = total.astype(BF16)
 
 
-def layout_kernel(ids, *refs):
+def layout_kernel(ids, sides, *refs):
     pieces = refs[:5]
     kern, back, maps = refs[5:]
 
@@ -526,43 +532,36 @@
     soon, late = ((0, 0), (0, 3), (1, 2)), ((0, 1), (1, 1))
     homes = soon + late
 
-    first_two = [
-        hop(packed, sizes, lambda s, d, r: (s, d ^ k, r) if (s, r) in homes else None)
-        for k in (1, 2)
-    ]
+    def across_groups(values, k, some):
+        return hop(values, sizes, lambda s, d, r: (s, d ^ k, r) if (s, r) in some else None)
+
+    first_two = [across_groups(packed, k, homes) for k in (1, 2)]
     mine = jnp.stack(
         [jnp.where(segment == 0, latent, decoder_in), jnp.where(segment == 0, hint, target)]
     )
     others = [hop(mine, sizes, lambda s, d, r: (s, d, r ^ k)) for k in (1, 2, 3)]
 
-    spare, point, packed, *others = lax.optimization_barrier(
-        (first_convs[0, 0], pointwise_weights[0, 0], packed, *others)
+    early = (packed, *first_two, across_groups(packed, 3, soon))
+    spare, point, *others = lax.optimization_barrier(
+        (first_convs[0, 0], pointwise_weights[0, 0], *others)
     )
     other = pack(spare, point)
-
-    def start(values, some):
-        return [
-            hop(values, sizes, lambda s, d, r: (s, d ^ k, r) if (s, r) in some else None)
-            for k in (1, 2)
-        ]
-
-    def complete(values, two, some):
-        inner = hop(
-            values, sizes, lambda s, d, r: (s, d ^ 3, r) if (s, r) in some and d in (1, 2) else None
-        )
-        outer = hop(
-            two[1], sizes, lambda s, d, r: (s, d ^ 1, r) if (s, r) in some and d in (1, 2) else None
-        )
-        return (values, *two, inner, outer)
-
-    more = start(other, ((1, 2),))
-    *first_two, direct = lax.optimization_barrier((*first_two, packed))
-    early = complete(direct, first_two, soon)
-    twice = jnp.logical_and(segment == 1, row == 2)
-    mixture = [jnp.where(twice, a, b) for a, b in ((other, direct), (more[1], first_two[1]))]
-    last = complete(mixture[0], [first_two[0], mixture[1]], late + ((1, 2),))
-    last = (direct, *first_two, *last[3:])
-    later = (other, *more, *last[3:])
+    later = [other, *(across_groups(other, k, ((1, 2),)) for k in (1, 2, 3))]
+    *first_two, direct, later[1], later[2] = lax.optimization_barrier(
+        (*first_two, packed, later[1], later[2])
+    )
+    last = (
+        direct,
+        *first_two,
+        hop(
+            direct, sizes, lambda s, d, r: (s, d ^ 3, r) if (s, r) in late and d in (1, 2) else None
+        ),
+        hop(
+            first_two[1],
+            sizes,
+            lambda s, d, r: (s, d ^ 1, r) if (s, r) in late and d in (1, 2) else None,
+        ),
+    )
 
     def one_hop(values, *moves):
         table = dict(moves)
@@ -573,14 +572,13 @@
 
         return hop(values, sizes, move)
 
-    images, sent, mixed, bend, sides = call(
+    images, sent, mixed, bend = call(
         functools.partial(early_kernel, width),
         [
             ((2,) + plane, BF16),
             ((2 * pair[0], pair[1]), BF16),
             (pair, BF16),
             (pair, BF16),
-            ((2 * pair[0], pair[1]), BF16),
         ],
         [kern, maps, wide],
         ids,
@@ -593,10 +591,19 @@
     below = one_hop(mixed, ((0, 0), (0, 2)))
     across = one_hop(mixed, ((0, 0), (0, 3)))
     bend = one_hop(bend, ((0, 0), (0, 1)))
+    (sides,) = call(
+        functools.partial(given_kernel, width),
+        [((2 * pair[0], pair[1]), BF16)],
+        [kern, maps, wide],
+        ids,
+        images,
+        *early,
+        work=us(3.5),
+    )
+    kernel, back, point = call(
+        layout_kernel, [kern, kern, maps], [], ids, sides, *last, work=us(2)
+    )
     sides = one_hop(sides, ((1, 2), (1, 1)))
-    kernel, back, point = call(
-        layout_kernel, [kern, kern, maps], [], ids, *last, work=us(2)
-    )
     kernel, point, near = lax.optimization_barrier((kernel, point, near))
     out, proj = call(
         functools.partial(middle_kernel, width),

time: 119 us -> 120 us (level)
  starting transfers between devices: 26.1 us -> 19.9 us
  blocking collectives: 14.4 us -> 18.7 us
  waiting for transfers between devices: 58.3 us -> 60.5 us
  local copies, waits for them, and re-layouts: 7.76 us -> 9.07 us
    ppermute x23, starting transfers between devices: 26.1 us -> 19.9 us  [hop(): return lax.ppermute(values, ('segment', 'dp', 'rows'), pairs)]
    all_to_all x1, blocking collectives: 14.4 us -> 18.7 us  [by_roles(): total = jnp.sum(lax.all_to_all(sent, 'dp', 0, 0).astype(F32), axis=0)]
    select_n x2 -> x0, other arithmetic: 2.19 us -> none  [by_roles(): jnp.where(twice, a, b)]
    ppermute x23, waiting for transfers between devices: 58.3 us -> 60.5 us  [hop(): return lax.ppermute(values, ('segment', 'dp', 'rows'), pairs)]
    slice x1 -> x0, local copies, waits for them, and re-layouts: 2.08 us -> none  [by_roles(): first_convs[0, 0]]
    dynamic_slice x1 -> x2, local copies, waits for them, and re-layouts: 0.28 us -> 2.31 us  [by_roles(): lax.dynamic_index_in_dim(first_convs[0], (row % 2 == 0).astype(jnp.int32)...]
    unnamed x24 -> x14, local copies, waits for them, and re-layouts: 3.63 us -> 4.98 us
    pallas_call x8 -> x9, Pallas kernels: 7.63 us -> 8.69 us  [call(): pl.pallas_call(body, out_shape=[jax.ShapeDtypeStruct(shape, dtype) for sh...]
  transfers between devices with their start and end apart: 23 -> 23, of which waited for: 5 -> 4; matrix products, arithmetic and copies ran while one was open for 1% -> 4% of each run, Pallas kernels for 5% -> 6%
where the time goes in v1:
time: 120 us
  waiting for transfers between devices  60.5 us (50%)
  starting transfers between devices  19.9 us (17%)
  blocking collectives  18.7 us (16%)
  local copies, waits for them, and re-layouts  9.07 us (8%)
  Pallas kernels  8.69 us (7%)
  other arithmetic  1.69 us (1%)
    ppermute x23, waiting for transfers between devices, hop(): return lax.ppermute(values, ('segment', 'dp', 'rows'), pairs)  60.5 us
    ppermute x23, starting transfers between devices, hop(): return lax.ppermute(values, ('segment', 'dp', 'rows'), pairs)  19.9 us
    all_to_all x1, blocking collectives, by_roles(): total = jnp.sum(lax.all_to_all(sent, 'dp', 0, 0).astype(F32), axis=0)  18.7 us
    pallas_call x9, Pallas kernels, call(): pl.pallas_call(body, out_shape=[jax.ShapeDtypeStruct(shape, dtype) for sh...  8.69 us
    unnamed x14, local copies, waits for them, and re-layouts  4.98 us
  transfers between devices with their start and end apart: 23, of which 4 were waited for; matrix products, arithmetic and copies ran while one was open for 4% of the time, Pallas kernels for 6%

profile of v1, /device:TPU:4, one launch (start us, length us, event | category | flops | bytes accessed | tf_op | source)
XLA Modules:
  0.0 119.6 jit_solution(1148370534955719697)
XLA Ops:
  0.6 1.0 select_bitcast_fusion
  1.7 1.6 %collective-permute-start = (bf16[2,2,4,16,320]{4,3,2,1,0:T(8,128)(2,1)S(1)}, bf16[2,2,4,16,320]{4,3,2,1,0:T(8,128)(2,1)S(1)}, u32[]{:S(2)}, u32[]{:S(2)}) collective-permute-start(bf16[2,2,4,16,320]{4,3,2,1,0:T(8,128)(2,1)S(1)} %pad_maximum_fusion.2.refs_0_), channel_id=1, source_target_pairs={{0,1},{1,0},{2,3},{3,2},{4,5},{5,4},{6,7},{7,6},{8,9},{9,8},{10,11... | collective-permute-start | bytes 491528 | tf_op jit(solution)/shard_map/ppermute | solution.py:482
  3.8 1.5 %collective-permute-start.2 = (bf16[2,2,4,16,320]{4,3,2,1,0:T(8,128)(2,1)S(1)}, bf16[2,2,4,16,320]{4,3,2,1,0:T(8,128)(2,1)S(1)}, u32[]{:S(2)}, u32[]{:S(2)}) collective-permute-start(bf16[2,2,4,16,320]{4,3,2,1,0:T(8,128)(2,1)S(1)} %pad_maximum_fusion.2.refs_0_), channel_id=1, source_target_pairs={{0,3},{1,2},{2,1},{3,0},{4,7},{5,6},{6,5},{7,4},{8,11},{9,10},{10,... | collective-permute-start | bytes 491528 | tf_op jit(solution)/shard_map/ppermute | solution.py:482
  5.3 2.0 %constant_dynamic-slice_fusion = (bf16[1,1,720,320]{2,3,1,0:T(8,128)(2,1)S(1)}, bf16[1,1,720,320]{2,3,1,0:T(8,128)(2,1)}) fusion(bf16[1,2,720,320]{2,3,1,0:T(8,128)(2,1)} %param.11, s32[]{:T(128)S(6)} %select_n.53), kind=kLoop, calls=%fused_computation.17 | loop fusion | bytes 1843204 | tf_op jit(solution)/shard_map/jit(dynamic_index_in_dim)/dynamic_slice | solution.py:521
  8.4 0.7 collective-permute-start.3
  9.1 0.7 collective-permute-start.4
  9.8 1.3 %copy.12 = bf16[1,1,720,320]{3,2,1,0:T(8,128)(2,1)S(1)} copy(bf16[1,1,720,320]{2,3,1,0:T(8,128)(2,1)} %get-tuple-element.66) | data formatting | bytes 921600
  11.1 2.7 %collective-permute-done.1.refs_2_ = bf16[2,2,4,16,320]{4,3,2,1,0:T(8,128)(2,1)S(1)} collective-permute-done((bf16[2,2,4,16,320]{4,3,2,1,0:T(8,128)(2,1)S(1)}, bf16[2,2,4,16,320]{4,3,2,1,0:T(8,128)(2,1)S(1)}, u32[]{:S(2)}, u32[]{:S(2)}) %collective-permute-start.1) | collective-permute-done | bytes 163872 | tf_op jit(solution)/shard_map/ppermute | solution.py:482
  15.4 0.7 collective-permute-start.6
  16.1 0.7 collective-permute-start.7
  16.8 1.5 %collective-permute-start.5 = (bf16[400,640]{1,0:T(8,128)(2,1)S(1)}, bf16[400,640]{1,0:T(8,128)(2,1)}, u32[]{:S(2)}, u32[]{:S(2)}) collective-permute-start(bf16[400,640]{1,0:T(8,128)(2,1)S(1)} %fusion.1.refs_4_.refs_0_), channel_id=1, source_target_pairs={{0,12},{3,15},{4,8},{7,11},{8,4},{11,7},{12,0},{15,3},{18,30},{22,... | collective-permute-start | bytes 1536008 | tf_op jit(solution)/shard_map/ppermute | solution.py:482
  18.4 0.7 collective-permute-start.8
  19.1 0.7 collective-permute-start.9
  19.8 0.9 copy-done.1
  20.7 0.9 copy-done.3
  21.7 1.1 shard_map.86
  22.8 0.7 collective-permute-start.10
  23.5 0.7 collective-permute-start.12
  24.2 1.1 shard_map.87.sides
  25.3 0.7 collective-permute-start.14
  26.0 0.7 shard_map.88
  29.3 1.3 %collective-permute-start.16 = (bf16[256,640]{1,0:T(8,128)(2,1)S(1)}, bf16[256,640]{1,0:T(8,128)(2,1)S(1)}, u32[]{:S(2)}, u32[]{:S(2)}) collective-permute-start(bf16[256,640]{1,0:T(8,128)(2,1)S(1)} %get-tuple-element.54.own), channel_id=1, source_target_pairs={{0,2},{4,6},{8,10},{12,14}} | collective-permute-start | bytes 983048 | tf_op jit(solution)/shard_map/ppermute | solution.py:482
  33.2 30.6 %collective-permute-done.16.below = bf16[256,640]{1,0:T(8,128)(2,1)S(1)} collective-permute-done((bf16[256,640]{1,0:T(8,128)(2,1)S(1)}, bf16[256,640]{1,0:T(8,128)(2,1)S(1)}, u32[]{:S(2)}, u32[]{:S(2)}) %collective-permute-start.16) | collective-permute-done | bytes 327712 | tf_op jit(solution)/shard_map/ppermute | solution.py:482
  63.8 2.1 %shard_map.92.chosen = bf16[4,2,96,512]{3,2,1,0:T(8,128)(2,1)S(1)} custom-call(s32[3]{0:T(128)S(1)} %pad_add_fusion.ids, bf16[256,640]{1,0:T(8,128)(2,1)S(1)} %get-tuple-element.54.own, bf16[512,640]{1,0:T(8,128)(2,1)S(1)} %collective-permute-done.10.near, bf16[256,640]{1,0:T(8,128)(2,1)S(1)} %collective-permute-done.16.below, ...), custom_call_target="tpu_custom_call" | custom-call | flops 2300000000 | tf_op jit(solution)/shard_map/pallas_call | solution.py:176
  66.6 0.7 collective-permute-start.19
  68.0 1.3 %collective-permute-start.21 = (bf16[320,640]{1,0:T(8,128)(2,1)S(1)}, bf16[320,640]{1,0:T(8,128)(2,1)S(1)}, u32[]{:S(2)}, u32[]{:S(2)}) collective-permute-start(bf16[320,640]{1,0:T(8,128)(2,1)S(1)} %get-tuple-element.62), channel_id=1, source_target_pairs={{1,2},{5,6},{9,10},{13,14}} | collective-permute-start | bytes 1228808 | tf_op jit(solution)/shard_map/ppermute | solution.py:482
  69.3 25.9 %collective-permute-done.21.third = bf16[320,640]{1,0:T(8,128)(2,1)S(1)} collective-permute-done((bf16[320,640]{1,0:T(8,128)(2,1)S(1)}, bf16[320,640]{1,0:T(8,128)(2,1)S(1)}, u32[]{:S(2)}, u32[]{:S(2)}) %collective-permute-start.21) | collective-permute-done | bytes 409632 | tf_op jit(solution)/shard_map/ppermute | solution.py:482
  95.3 1.4 %shard_map.94 = (bf16[4,64,640]{2,1,0:T(8,128)(2,1)S(1)}, bf16[4,64,640]{2,1,0:T(8,128)(2,1)S(1)}) custom-call(s32[3]{0:T(128)S(1)} %pad_add_fusion.ids, bf16[4,2,96,512]{3,2,1,0:T(8,128)(2,1)S(1)} %shard_map.92.chosen, bf16[4,320,640]{2,1,0:T(8,128)(2,1)S(1)} %shard_map.93.parcel, bf16[320,640]{1,0:T(8,128)(2,1)S(1)} %collective-permute-done.19.first, ...), custom_call_target="tpu_custom_call" | custom-call | tf_op jit(solution)/shard_map/pallas_call | solution.py:176
  96.7 1.3 %collective-permute-start.22 = (bf16[4,64,640]{2,1,0:T(8,128)(2,1)S(1)}, bf16[4,64,640]{2,1,0:T(8,128)(2,1)S(1)}, u32[]{:S(2)}, u32[]{:S(2)}) collective-permute-start(bf16[4,64,640]{2,1,0:T(8,128)(2,1)S(1)} %get-tuple-element.61), channel_id=1, source_target_pairs={{0,16},{1,17},{2,18},{3,19},{4,20},{5,21},{6,22},{7,23},{8,24},{9,... | collective-permute-start | bytes 983048 | tf_op jit(solution)/shard_map/ppermute | solution.py:482
  98.0 1.2 %collective-permute-done.22 = bf16[4,64,640]{2,1,0:T(8,128)(2,1)S(1)} collective-permute-done((bf16[4,64,640]{2,1,0:T(8,128)(2,1)S(1)}, bf16[4,64,640]{2,1,0:T(8,128)(2,1)S(1)}, u32[]{:S(2)}, u32[]{:S(2)}) %collective-permute-start.22) | collective-permute-done | bytes 327712 | tf_op jit(solution)/shard_map/ppermute | solution.py:482
  99.3 18.7 %all_to_all.5 = bf16[4,64,640]{2,1,0:T(8,128)(2,1)S(1)} all-to-all(bf16[4,64,640]{2,1,0:T(8,128)(2,1)S(1)} %broadcast_select_fusion), channel_id=1, replica_groups=mesh['segment'=2,'dp'=4,'rows'=4] {'dp'}, dimensions={0} | all-to-all | bytes 655360 | tf_op jit(solution)/shard_map/all_to_all | solution.py:686
  118.2 0.8 slice.67
  (58 shorter events, 10.7 us)
Async XLA Ops:
  0.6 7.0 %copy-start.4 = (bf16[1,720,320]{1,2,0:T(8,128)(2,1)S(1)}, bf16[1,720,320]{1,2,0:T(8,128)(2,1)}, u32[]{:S(2)}) copy-start(bf16[1,720,320]{1,2,0:T(8,128)(2,1)} %param.12) | copy-start | bytes 1382404
  1.7 9.4 %collective-permute-start = (bf16[2,2,4,16,320]{4,3,2,1,0:T(8,128)(2,1)S(1)}, bf16[2,2,4,16,320]{4,3,2,1,0:T(8,128)(2,1)S(1)}, u32[]{:S(2)}, u32[]{:S(2)}) collective-permute-start(bf16[2,2,4,16,320]{4,3,2,1,0:T(8,128)(2,1)S(1)} %pad_maximum_fusion.2.refs_0_), channel_id=1, source_target_pairs={{0,1},{1,0},{2,3},{3,2},{4,5},{5,4},{6,7},{7,6},{8,9},{9,8},{10,11... | collective-permute-start | bytes 491528 | tf_op jit(solution)/shard_map/ppermute | solution.py:482
  3.3 10.6 %collective-permute-start.1 = (bf16[2,2,4,16,320]{4,3,2,1,0:T(8,128)(2,1)S(1)}, bf16[2,2,4,16,320]{4,3,2,1,0:T(8,128)(2,1)S(1)}, u32[]{:S(2)}, u32[]{:S(2)}) collective-permute-start(bf16[2,2,4,16,320]{4,3,2,1,0:T(8,128)(2,1)S(1)} %pad_maximum_fusion.2.refs_0_), channel_id=1, source_target_pairs={{0,2},{1,3},{2,0},{3,1},{4,6},{5,7},{6,4},{7,5},{8,10},{9,11},{10,... | collective-permute-start | bytes 491528 | tf_op jit(solution)/shard_map/ppermute | solution.py:482
  3.8 10.8 %collective-permute-start.2 = (bf16[2,2,4,16,320]{4,3,2,1,0:T(8,128)(2,1)S(1)}, bf16[2,2,4,16,320]{4,3,2,1,0:T(8,128)(2,1)S(1)}, u32[]{:S(2)}, u32[]{:S(2)}) collective-permute-start(bf16[2,2,4,16,320]{4,3,2,1,0:T(8,128)(2,1)S(1)} %pad_maximum_fusion.2.refs_0_), channel_id=1, source_target_pairs={{0,3},{1,2},{2,1},{3,0},{4,7},{5,6},{6,5},{7,4},{8,11},{9,10},{10,... | collective-permute-start | bytes 491528 | tf_op jit(solution)/shard_map/ppermute | solution.py:482
  7.3 0.9 copy-start.5
  8.4 10.0 %collective-permute-start.3 = (bf16[400,640]{1,0:T(8,128)(2,1)S(1)}, bf16[400,640]{1,0:T(8,128)(2,1)S(1)}, u32[]{:S(2)}, u32[]{:S(2)}) collective-permute-start(bf16[400,640]{1,0:T(8,128)(2,1)S(1)} %fusion.1.refs_4_.refs_0_), channel_id=1, source_target_pairs={{0,4},{1,5},{3,7},{4,0},{5,1},{7,3},{8,12},{9,13},{11,15},{12,8},{... | collective-permute-start | bytes 1536008 | tf_op jit(solution)/shard_map/ppermute | solution.py:482
  9.1 9.3 %collective-permute-start.4 = (bf16[400,640]{1,0:T(8,128)(2,1)S(1)}, bf16[400,640]{1,0:T(8,128)(2,1)S(1)}, u32[]{:S(2)}, u32[]{:S(2)}) collective-permute-start(bf16[400,640]{1,0:T(8,128)(2,1)S(1)} %fusion.1.refs_4_.refs_0_), channel_id=1, source_target_pairs={{0,8},{1,9},{3,11},{4,12},{5,13},{7,15},{8,0},{9,1},{11,3},{12,4},... | collective-permute-start | bytes 1536008 | tf_op jit(solution)/shard_map/ppermute | solution.py:482
  13.9 0.7 copy-start
  14.5 0.7 copy-start.2
  15.4 2.9 %collective-permute-start.6 = (bf16[400,640]{1,0:T(8,128)(2,1)S(1)}, bf16[400,640]{1,0:T(8,128)(2,1)S(1)}, u32[]{:S(2)}, u32[]{:S(2)}) collective-permute-start(bf16[400,640]{1,0:T(8,128)(2,1)S(1)} %fusion.refs_0_), channel_id=1, source_target_pairs={{18,22},{22,18},{26,30},{30,26}} | collective-permute-start | bytes 1536008 | tf_op jit(solution)/shard_map/ppermute | solution.py:482
  16.1 2.2 %collective-permute-start.7 = (bf16[400,640]{1,0:T(8,128)(2,1)S(1)}, bf16[400,640]{1,0:T(8,128)(2,1)S(1)}, u32[]{:S(2)}, u32[]{:S(2)}) collective-permute-start(bf16[400,640]{1,0:T(8,128)(2,1)S(1)} %fusion.refs_0_), channel_id=1, source_target_pairs={{18,26},{22,30},{26,18},{30,22}} | collective-permute-start | bytes 1536008 | tf_op jit(solution)/shard_map/ppermute | solution.py:482
  16.8 3.0 %collective-permute-start.5 = (bf16[400,640]{1,0:T(8,128)(2,1)S(1)}, bf16[400,640]{1,0:T(8,128)(2,1)}, u32[]{:S(2)}, u32[]{:S(2)}) collective-permute-start(bf16[400,640]{1,0:T(8,128)(2,1)S(1)} %fusion.1.refs_4_.refs_0_), channel_id=1, source_target_pairs={{0,12},{3,15},{4,8},{7,11},{8,4},{11,7},{12,0},{15,3},{18,30},{22,... | collective-permute-start | bytes 1536008 | tf_op jit(solution)/shard_map/ppermute | solution.py:482
  18.4 7.6 %collective-permute-start.8 = (bf16[400,640]{1,0:T(8,128)(2,1)S(1)}, bf16[400,640]{1,0:T(8,128)(2,1)S(1)}, u32[]{:S(2)}, u32[]{:S(2)}) collective-permute-start(bf16[400,640]{1,0:T(8,128)(2,1)S(1)} %fusion.1.refs_4_.refs_0_), channel_id=1, source_target_pairs={{5,9},{9,5},{21,25},{25,21}} | collective-permute-start | bytes 1536008 | tf_op jit(solution)/shard_map/ppermute | solution.py:482
  19.1 6.9 %collective-permute-start.9 = (bf16[400,640]{1,0:T(8,128)(2,1)S(1)}, bf16[400,640]{1,0:T(8,128)(2,1)S(1)}, u32[]{:S(2)}, u32[]{:S(2)}) collective-permute-start(bf16[400,640]{1,0:T(8,128)(2,1)S(1)} %collective-permute-done.4.refs_6_.refs_2_), channel_id=1, source_target_pairs={{5,1},{9,13},{21,17},{25,29}} | collective-permute-start | bytes 1536008 | tf_op jit(solution)/shard_map/ppermute | solution.py:482
  19.8 0.9 copy-start.1
  20.7 0.9 copy-start.3
  22.8 4.0 %collective-permute-start.10 = (bf16[512,640]{1,0:T(8,128)(2,1)S(1)}, bf16[512,640]{1,0:T(8,128)(2,1)S(1)}, u32[]{:S(2)}, u32[]{:S(2)}) collective-permute-start(bf16[512,640]{1,0:T(8,128)(2,1)S(1)} %get-tuple-element.43), channel_id=1, source_target_pairs={{0,1},{3,18},{4,5},{7,22},{8,9},{11,26},{12,13},{15,30}} | collective-permute-start | bytes 1966088 | tf_op jit(solution)/shard_map/ppermute | solution.py:482
  23.5 3.8 %collective-permute-start.12 = (bf16[400,640]{1,0:T(8,128)(2,1)S(1)}, bf16[400,640]{1,0:T(8,128)(2,1)S(1)}, u32[]{:S(2)}, u32[]{:S(2)}) collective-permute-start(bf16[400,640]{1,0:T(8,128)(2,1)S(1)} %fusion.refs_0_), channel_id=1, source_target_pairs={{18,30},{22,26},{26,22},{30,18}} | collective-permute-start | bytes 1536008 | tf_op jit(solution)/shard_map/ppermute | solution.py:482
  25.3 6.0 %collective-permute-start.14 = (bf16[512,640]{1,0:T(8,128)(2,1)S(1)}, bf16[512,640]{1,0:T(8,128)(2,1)S(1)}, u32[]{:S(2)}, u32[]{:S(2)}) collective-permute-start(bf16[512,640]{1,0:T(8,128)(2,1)S(1)} %shard_map.87.sides), channel_id=1, source_target_pairs={{18,17},{22,21},{26,25},{30,29}} | collective-permute-start | bytes 1966088 | tf_op jit(solution)/shard_map/ppermute | solution.py:482
  27.9 3.4 %collective-permute-start.13 = (bf16[256,640]{1,0:T(8,128)(2,1)S(1)}, bf16[256,640]{1,0:T(8,128)(2,1)S(1)}, u32[]{:S(2)}, u32[]{:S(2)}) collective-permute-start(bf16[256,640]{1,0:T(8,128)(2,1)S(1)} %shard_map.90), channel_id=1, source_target_pairs={{18,17},{22,21},{26,25},{30,29}} | collective-permute-start | bytes 983048 | tf_op jit(solution)/shard_map/ppermute | solution.py:482
  28.6 2.7 %collective-permute-start.11 = (bf16[256,640]{1,0:T(8,128)(2,1)S(1)}, bf16[256,640]{1,0:T(8,128)(2,1)S(1)}, u32[]{:S(2)}, u32[]{:S(2)}) collective-permute-start(bf16[256,640]{1,0:T(8,128)(2,1)S(1)} %get-tuple-element.48), channel_id=1, source_target_pairs={{1,17},{5,21},{9,25},{13,29}} | collective-permute-start | bytes 983048 | tf_op jit(solution)/shard_map/ppermute | solution.py:482
  29.3 34.5 %collective-permute-start.16 = (bf16[256,640]{1,0:T(8,128)(2,1)S(1)}, bf16[256,640]{1,0:T(8,128)(2,1)S(1)}, u32[]{:S(2)}, u32[]{:S(2)}) collective-permute-start(bf16[256,640]{1,0:T(8,128)(2,1)S(1)} %get-tuple-element.54.own), channel_id=1, source_target_pairs={{0,2},{4,6},{8,10},{12,14}} | collective-permute-start | bytes 983048 | tf_op jit(solution)/shard_map/ppermute | solution.py:482
  30.6 33.2 %collective-permute-start.17 = (bf16[256,640]{1,0:T(8,128)(2,1)S(1)}, bf16[256,640]{1,0:T(8,128)(2,1)S(1)}, u32[]{:S(2)}, u32[]{:S(2)}) collective-permute-start(bf16[256,640]{1,0:T(8,128)(2,1)S(1)} %get-tuple-element.54.own), channel_id=1, source_target_pairs={{0,3},{4,7},{8,11},{12,15}} | collective-permute-start | bytes 983048 | tf_op jit(solution)/shard_map/ppermute | solution.py:482
  31.8 34.1 %collective-permute-start.15 = (bf16[256,640]{1,0:T(8,128)(2,1)S(1)}, bf16[256,640]{1,0:T(8,128)(2,1)S(1)}, u32[]{:S(2)}, u32[]{:S(2)}) collective-permute-start(bf16[256,640]{1,0:T(8,128)(2,1)S(1)} %get-tuple-element.53), channel_id=1, source_target_pairs={{17,1},{21,5},{25,9},{29,13}} | collective-permute-start | bytes 983048 | tf_op jit(solution)/shard_map/ppermute | solution.py:482
  32.5 33.4 %collective-permute-start.18 = (bf16[256,640]{1,0:T(8,128)(2,1)S(1)}, bf16[256,640]{1,0:T(8,128)(2,1)S(1)}, u32[]{:S(2)}, u32[]{:S(2)}) collective-permute-start(bf16[256,640]{1,0:T(8,128)(2,1)S(1)} %get-tuple-element.57), channel_id=1, source_target_pairs={{0,1},{4,5},{8,9},{12,13}} | collective-permute-start | bytes 983048 | tf_op jit(solution)/shard_map/ppermute | solution.py:482
  66.6 2.7 %collective-permute-start.19 = (bf16[320,640]{1,0:T(8,128)(2,1)S(1)}, bf16[320,640]{1,0:T(8,128)(2,1)S(1)}, u32[]{:S(2)}, u32[]{:S(2)}) collective-permute-start(bf16[320,640]{1,0:T(8,128)(2,1)S(1)} %get-tuple-element.64), channel_id=1, source_target_pairs={{1,0},{5,4},{9,8},{13,12}} | collective-permute-start | bytes 1228808 | tf_op jit(solution)/shard_map/ppermute | solution.py:482
  67.3 2.0 %collective-permute-start.20 = (bf16[320,640]{1,0:T(8,128)(2,1)S(1)}, bf16[320,640]{1,0:T(8,128)(2,1)S(1)}, u32[]{:S(2)}, u32[]{:S(2)}) collective-permute-start(bf16[320,640]{1,0:T(8,128)(2,1)S(1)} %get-tuple-element.63), channel_id=1, source_target_pairs={{1,3},{5,7},{9,11},{13,15}} | collective-permute-start | bytes 1228808 | tf_op jit(solution)/shard_map/ppermute | solution.py:482
  68.0 27.3 %collective-permute-start.21 = (bf16[320,640]{1,0:T(8,128)(2,1)S(1)}, bf16[320,640]{1,0:T(8,128)(2,1)S(1)}, u32[]{:S(2)}, u32[]{:S(2)}) collective-permute-start(bf16[320,640]{1,0:T(8,128)(2,1)S(1)} %get-tuple-element.62), channel_id=1, source_target_pairs={{1,2},{5,6},{9,10},{13,14}} | collective-permute-start | bytes 1228808 | tf_op jit(solution)/shard_map/ppermute | solution.py:482
  96.7 2.5 %collective-permute-start.22 = (bf16[4,64,640]{2,1,0:T(8,128)(2,1)S(1)}, bf16[4,64,640]{2,1,0:T(8,128)(2,1)S(1)}, u32[]{:S(2)}, u32[]{:S(2)}) collective-permute-start(bf16[4,64,640]{2,1,0:T(8,128)(2,1)S(1)} %get-tuple-element.61), channel_id=1, source_target_pairs={{0,16},{1,17},{2,18},{3,19},{4,20},{5,21},{6,22},{7,23},{8,24},{9,... | collective-permute-start | bytes 983048 | tf_op jit(solution)/shard_map/ppermute | solution.py:482
